TPU v7x, 32 devices: a whole 2x2x4 slice. The times are simulated.
32 devices in a mesh: groups: 2 (over x), kel: 16 (over z, y, core).
Axes of the slice: x: 2, y: 2, z: 4, core: 2. Of those that a mesh axis runs over, the one named last changes fastest.
Arguments:
- electrons: float32 [32, 8, 64], P(('groups', 'kel')), parts along dimension 0, may hold values from 0 to 1
- phonons: float32 [64, 6, 64], P(('groups', 'kel')), parts along dimension 0, may hold values from 0 to 2
- elec_wannier: bfloat16 [32, 256, 64], P(('groups', 'kel')), parts along dimension 0, may hold values from -6 to 6
- phon_wannier: bfloat16 [64, 256, 64], P(('groups', 'kel')), parts along dimension 0, may hold values from -0.375 to 0.375
- coupling: bfloat16 [48, 256, 256], replicated, may hold values from -0.375 to 0.375
- pair_blocks: int32 [32, 12], P(('groups', 'kel')), parts along dimension 0, may hold values from 0 to 31, as said below
- pair_counts: int32 [32], P(('groups', 'kel')), parts along dimension 0, may hold values from 1 to 12, as said below
- drift_speed: float32 [16], P('groups'), parts along dimension 0, may hold values from 0.2 to 0.8
Outputs:
- electrons_out: float32 [32, 8, 64], P(('groups', 'kel')), parts along dimension 0
- phonons_out: float32 [64, 6, 64], P(('groups', 'kel')), parts along dimension 0
There are 2 independent parts, one for each index of `groups`. A program takes and returns all parts, laid end to end along the dimension named above; an argument that names none is the same for every part. Nothing has to cross between parts.
Inputs may be any that keep to these rules, and one draw needn't show every extreme that they name: `pair_blocks`: within one kx plane the 12 q-blocks are distinct. `pair_counts`: some kx plane has all 12 slots live.
All inputs are finite; a program needn't handle non-finite values.
Results may differ from a plain program's by a relative error of at most 0.0015.
Values may be sent and summed in bfloat16 or wider, within the bound.
A program may use at most 64 MiB of HBM per device.

v0:
```python
import jax
import jax.numpy as jnp
from jax import lax
from jax.sharding import PartitionSpec as P

STEPS = 2


step_length = 0.5


def shifted(value, axis, steps):
    count = lax.axis_size(axis)
    pairs = [(source, (source + steps) % count) for source in range(count)]
    return lax.ppermute(value, axis, pairs)


def body(
    electrons, phonons, elec_wannier, phon_wannier, coupling, pair_blocks, pair_counts, drift_speed
):
    hp = lax.Precision.HIGHEST
    planes, bands, kpoints = electrons.shape
    qblocks, modes, qpoints = phonons.shape
    slots = pair_blocks.shape[1]
    total_blocks = qblocks * lax.axis_size("kel")
    items = planes * slots
    flat_ids = pair_blocks.reshape(-1)
    plane_of = jnp.arange(items, dtype=jnp.int32) // slots
    valid = (jnp.arange(slots)[None, :] < pair_counts[:, None]).reshape(-1)
    amp = jnp.einsum(
        "xri,crs->xcis", elec_wannier, coupling, preferred_element_type=jnp.float32
    ).astype(jnp.bfloat16)
    all_feats = lax.all_gather(phon_wannier, "kel", axis=0, tiled=True)
    chosen_feats = all_feats[flat_ids]

    def squared(item):
        field = jnp.einsum(
            "cis,sj->cij",
            amp[plane_of[item]],
            chosen_feats[item],
            preferred_element_type=jnp.float32,
        )
        return field * field

    def couple(item):
        return jnp.where(valid[item], squared(item), 0.0).astype(jnp.bfloat16)

    strength = lax.map(couple, jnp.arange(items))

    def table_of(item):
        return strength[item]

    def rates(occ_e, occ_n):
        every_n = lax.all_gather(occ_n, "kel", axis=0, tiled=True)
        chosen_n = every_n[flat_ids]
        rim = shifted(occ_e, "kel", 1)
        previous = jnp.concatenate([rim, occ_e[:-1]], axis=0)

        def item_rates(item):
            table = table_of(item).astype(jnp.float32).reshape(bands, modes, kpoints, qpoints)
            occ_plane = occ_e[plane_of[item]]
            chosen = chosen_n[item]
            upper = jnp.einsum("bmij,mj->bi", table, 1.0 + 2.0 * chosen, precision=hp)
            lower = jnp.einsum("bmij,mj->bi", table, chosen, precision=hp)
            toward = jnp.einsum("bmij,bi->mj", table, occ_plane, precision=hp)
            plain = jnp.sum(table, axis=(0, 2))
            return (occ_plane * upper - lower, (1.0 + 2.0 * chosen) * toward - chosen * plain)

        loss, gained = lax.map(item_rates, jnp.arange(items))
        loss = jnp.sum(loss.reshape(planes, slots, bands, kpoints), axis=1)
        onehot = (flat_ids[:, None] == jnp.arange(total_blocks)[None, :]).astype(jnp.float32)
        dense = jnp.einsum("kq,kmj->qmj", onehot, gained, precision=hp)
        mine = lax.psum_scatter(dense, "kel", scatter_dimension=0, tiled=True)
        rate_e = -loss / (slots * modes * qpoints) - drift_speed[None, :, None] * (occ_e - previous)
        rate_n = mine / (slots * bands * kpoints)
        return (rate_e, rate_n)

    occ_e, occ_n = (electrons, phonons)
    for step in range(STEPS):
        first_e, first_n = rates(occ_e, occ_n)
        second_e, second_n = rates(occ_e + step_length * first_e, occ_n + step_length * first_n)
        occ_e = occ_e + 0.5 * step_length * (first_e + second_e)
        occ_n = occ_n + 0.5 * step_length * (first_n + second_n)
    return (occ_e, occ_n)


def solution(mesh):
    placed = (
        P(("groups", "kel"), None, None),
        P(("groups", "kel"), None, None),
        P(("groups", "kel"), None, None),
        P(("groups", "kel"), None, None),
        P(),
        P(("groups", "kel"), None),
        P(("groups", "kel")),
        P("groups"),
    )
    return jax.shard_map(
        body,
        mesh=mesh,
        in_specs=placed,
        out_specs=(P(("groups", "kel"), None, None), P(("groups", "kel"), None, None)),
        check_vma=False,
    )
```

profile of v0, /device:TPU:0, one launch (start us, length us, event | category | flops | bytes accessed | tf_op | source)
XLA Modules:
  0.0 820.3 jit_solution(18060557280538664276)
XLA Ops:
  9.8 23.1 %all_gather.16 = f32[32,6,64]{2,1,0:T(8,128)S(1)} all-gather(f32[2,6,64]{2,1,0:T(8,128)S(1)} %copy.33), channel_id=1, replica_groups=mesh['groups'=2,'kel'=16] {'kel'}, dimensions={0}, use_global_device_ids=true | all-gather | bytes 52224 | tf_op jit(solution)/shard_map/all_gather | solution.py:54
  35.9 4.1 fusion.45
  40.0 10.8 %all-gather.2.cloned.1.call-done = bf16[32,256,64]{1,2,0:T(8,128)(2,1)} async-done(((bf16[2,256,64]{1,2,0:T(8,128)(2,1)}), bf16[32,256,64]{1,2,0:T(8,128)(2,1)}) %all-gather.2.cloned.1.call-update) | async-done | bytes 1048592 | tf_op jit(solution)/shard_map/all_gather | solution.py:33
  50.9 2.6 gather_fusion
  53.4 81.9 %while.63 = (s32[]{:T(128)}, bf16[12,48,64,64]{3,2,1,0:T(8,128)(2,1)}, s32[12]{0:T(128)S(1)}, pred[12]{0:T(512)(128)(4,1)S(1)}, bf16[12,256,64]{1,2,0:T(8,128)(2...) while((s32[]{:T(128)}, bf16[12,48,64,64]{3,2,1,0:T(8,128)(2,1)}, ...), condition=%wide.region_1.2_spmd, body=%wide.region_0.1_spmd.sunk | while | flops 101253120 | bytes 3966101 | solution.py:48
  56.6 2.3 fusion.141
  63.4 2.3 fusion.141
  70.2 2.3 fusion.141
  77.0 2.3 fusion.141
  83.9 2.3 fusion.141
  90.7 2.3 fusion.141
  97.5 2.3 fusion.141
  104.3 2.3 fusion.141
  111.1 2.3 fusion.141
  117.9 2.3 fusion.141
  124.7 2.3 fusion.141
  131.6 2.3 fusion.141
  135.4 80.0 %while.64 = (s32[]{:T(128)}, f32[12,8,64]{2,1,0:T(8,128)S(1)}, f32[12,6,64]{2,0,1:T(8,128)S(1)}, f32[1,8,64]{2,1,0:T(8,128)S(1)}, s32[12]{0:T(128)S(1)}, /*index...) while((s32[]{:T(128)}, f32[12,8,64]{2,1,0:T(8,128)S(1)}, ...), condition=%wide.region_5.6_spmd, body=%wide.region_2.5_spmd.sunk | while | flops 7473669 | bytes 2060979 | solution.py:69
  215.7 60.4 %all-reduce = f32[32,6,64]{2,0,1:T(8,128)S(1)} all-reduce(f32[32,6,64]{2,0,1:T(8,128)S(1)} %fusion.54), channel_id=2, replica_groups=mesh['groups'=2,'kel'=16] {'kel'}, use_global_device_ids=true, to_apply=%region_7.8.clone | all-reduce | flops 12288 | bytes 98304
  276.2 17.5 %all_gather.17 = f32[32,6,64]{2,1,0:T(8,128)S(1)} all-gather(f32[2,6,64]{2,1,0:T(8,128)S(1)} %copy.36), channel_id=1, replica_groups=mesh['groups'=2,'kel'=16] {'kel'}, dimensions={0}, use_global_device_ids=true | all-gather | bytes 52224 | tf_op jit(solution)/shard_map/all_gather | solution.py:54
  295.3 96.2 %while.65 = (s32[]{:T(128)}, f32[12,8,64]{2,1,0:T(8,128)S(1)}, f32[12,6,64]{2,0,1:T(8,128)S(1)}, f32[1,8,64]{2,1,0:T(8,128)}, s32[12]{0:T(128)S(1)}, /*index=5*/...) while((s32[]{:T(128)}, f32[12,8,64]{2,1,0:T(8,128)S(1)}, ...), condition=%wide.region_11.12_spmd, body=%wide.region_8.11_spmd.sunk | while | flops 7473669 | bytes 2058931 | solution.py:69
  391.8 62.4 %all-reduce.1 = f32[32,6,64]{2,0,1:T(8,128)S(1)} all-reduce(f32[32,6,64]{2,0,1:T(8,128)S(1)} %fusion.52), channel_id=3, replica_groups=mesh['groups'=2,'kel'=16] {'kel'}, use_global_device_ids=true, to_apply=%region_13.14.clone | all-reduce | flops 12288 | bytes 98304
  454.3 17.5 %all_gather.18 = f32[32,6,64]{2,1,0:T(8,128)S(1)} all-gather(f32[2,6,64]{2,1,0:T(8,128)S(1)} %copy.39), channel_id=1, replica_groups=mesh['groups'=2,'kel'=16] {'kel'}, dimensions={0}, use_global_device_ids=true | all-gather | bytes 52224 | tf_op jit(solution)/shard_map/all_gather | solution.py:54
  473.4 96.4 %while.66 = (s32[]{:T(128)}, f32[12,8,64]{2,1,0:T(8,128)S(1)}, f32[12,6,64]{2,0,1:T(8,128)S(1)}, f32[1,8,64]{2,1,0:T(8,128)}, s32[12]{0:T(128)S(1)}, /*index=5*/...) while((s32[]{:T(128)}, f32[12,8,64]{2,1,0:T(8,128)S(1)}, ...), condition=%wide.region_17.18_spmd, body=%wide.region_14.17_spmd.sunk | while | flops 7473669 | bytes 2058931 | solution.py:69
  570.2 62.4 %all-reduce.2 = f32[32,6,64]{2,0,1:T(8,128)S(1)} all-reduce(f32[32,6,64]{2,0,1:T(8,128)S(1)} %fusion.50), channel_id=4, replica_groups=mesh['groups'=2,'kel'=16] {'kel'}, use_global_device_ids=true, to_apply=%region_19.20.clone | all-reduce | flops 12288 | bytes 98304
  632.6 17.5 %all_gather.19 = f32[32,6,64]{2,1,0:T(8,128)S(1)} all-gather(f32[2,6,64]{2,1,0:T(8,128)S(1)} %copy.42), channel_id=1, replica_groups=mesh['groups'=2,'kel'=16] {'kel'}, dimensions={0}, use_global_device_ids=true | all-gather | bytes 52224 | tf_op jit(solution)/shard_map/all_gather | solution.py:54
  652.4 96.3 %while.67 = (s32[]{:T(128)}, f32[12,8,64]{2,1,0:T(8,128)S(1)}, f32[12,6,64]{2,0,1:T(8,128)S(1)}, f32[1,8,64]{2,1,0:T(8,128)}, s32[12]{0:T(128)S(1)}, /*index=5*/...) while((s32[]{:T(128)}, f32[12,8,64]{2,1,0:T(8,128)S(1)}, ...), condition=%wide.region_23.24_spmd, body=%wide.region_20.23_spmd.sunk | while | flops 7473669 | bytes 2058931 | solution.py:69
  663.0 1.5 convert_reduce_fusion.11
  671.0 1.5 convert_reduce_fusion.11
  679.1 1.5 convert_reduce_fusion.11
  687.1 1.5 convert_reduce_fusion.11
  749.0 62.4 %all-reduce.3 = f32[32,6,64]{2,0,1:T(8,128)S(1)} all-reduce(f32[32,6,64]{2,0,1:T(8,128)S(1)} %fusion.48), channel_id=5, replica_groups=mesh['groups'=2,'kel'=16] {'kel'}, use_global_device_ids=true, to_apply=%region_25.26.clone | all-reduce | flops 12288 | bytes 98304
  (682 shorter events, 311.3 us)
Async XLA Ops:
  7.2 28.7 %copy-start = (bf16[1,256,64]{1,2,0:T(8,128)(2,1)S(1)}, bf16[1,256,64]{1,2,0:T(8,128)(2,1)}, u32[]{:S(2)}) copy-start(bf16[1,256,64]{1,2,0:T(8,128)(2,1)} %param.20) | copy-start | bytes 98308
  7.2 43.7 %all-gather.2.cloned.1.call-start = ((), (), s32[]{:S(2)}) async-start(), calls=%async_computation | async-start | bytes 1114112 | tf_op jit(solution)/shard_map/all_gather | solution.py:33
  7.9 286.4 %collective-permute-start = (f32[1,8,64]{2,1,0:T(8,128)}, f32[1,8,64]{2,1,0:T(8,128)S(1)}, u32[]{:S(2)}, u32[]{:S(2)}) collective-permute-start(f32[1,8,64]{2,1,0:T(8,128)} %param.18), channel_id=1, source_target_pairs={{0,1},{1,2},{2,3},{3,4},{4,5},{5,6},{6,7},{7,8},{8,9},{9,10},{10,1... | collective-permute-start | bytes 6152 | tf_op jit(solution)/shard_map/ppermute | solution.py:15
  53.4 81.9 %copy-start.1 = (f32[1,8,64]{2,1,0:T(8,128)S(1)}, f32[1,8,64]{2,1,0:T(8,128)}, u32[]{:S(2)}) copy-start(f32[1,8,64]{2,1,0:T(8,128)} %param.18) | copy-start | bytes 6148
  135.4 80.1 %copy-start.3 = (s32[1,12]{1,0:T(1,128)S(1)}, s32[1,12]{1,0:T(1,128)}, u32[]{:S(2)}) copy-start(s32[1,12]{1,0:T(1,128)} %param.23) | copy-start | bytes 148
  135.4 140.8 %copy-start.2 = (f32[2,6,64]{2,0,1:T(2,128)S(1)}, f32[2,6,64]{2,0,1:T(2,128)}, u32[]{:S(2)}) copy-start(f32[2,6,64]{2,0,1:T(2,128)} %param.19) | copy-start | bytes 9220
  135.4 158.9 %copy-start.4 = (f32[8]{0:T(128)S(1)}, f32[8]{0:T(128)}, u32[]{:S(2)}) copy-start(f32[8]{0:T(128)} %param.25) | copy-start | bytes 100
  295.0 177.4 %collective-permute-start.1 = (f32[1,8,64]{2,1,0:T(8,128)}, f32[1,8,64]{2,1,0:T(8,128)S(1)}, u32[]{:S(2)}, u32[]{:S(2)}) collective-permute-start(f32[1,8,64]{2,1,0:T(8,128)} %multiply_add_fusion.3), channel_id=1, source_target_pairs={{0,1},{1,2},{2,3},{3,4},{4,5},{5,6},{6,7},{7,8},{8,9},{9,10},{10,1... | collective-permute-start | bytes 6152 | tf_op jit(solution)/shard_map/ppermute | solution.py:15
  473.1 177.6 %collective-permute-start.2 = (f32[1,8,64]{2,1,0:T(8,128)}, f32[1,8,64]{2,1,0:T(8,128)S(1)}, u32[]{:S(2)}, u32[]{:S(2)}) collective-permute-start(f32[1,8,64]{2,1,0:T(8,128)} %fusion.65), channel_id=1, source_target_pairs={{0,1},{1,2},{2,3},{3,4},{4,5},{5,6},{6,7},{7,8},{8,9},{9,10},{10,1... | collective-permute-start | bytes 6152 | tf_op jit(solution)/shard_map/ppermute | solution.py:15
  652.1 160.0 %collective-permute-start.3 = (f32[1,8,64]{2,1,0:T(8,128)}, f32[1,8,64]{2,1,0:T(8,128)S(1)}, u32[]{:S(2)}, u32[]{:S(2)}) collective-permute-start(f32[1,8,64]{2,1,0:T(8,128)} %multiply_add_fusion.2), channel_id=1, source_target_pairs={{0,1},{1,2},{2,3},{3,4},{4,5},{5,6},{6,7},{7,8},{8,9},{9,10},{10,1... | collective-permute-start | bytes 6152 | tf_op jit(solution)/shard_map/ppermute | solution.py:15
Sparse Core Ops, SparseCore 0:
  10.2 40.6 all-gather.1
where the time goes:
time: 828 us; the launch traced here: 820 us
  blocking collectives  323 us (39%)
  matrix products  175 us (21%)
  loops' own time  119 us (14%)
  other arithmetic  105 us (13%)
  local copies, waits for them, and re-layouts  69.5 us (8%)
  between operations  15.5 us (2%)
  waiting for transfers between devices  11.5 us (1%)
    unnamed x4, blocking collectives  248 us
    another operation x4, loops' own time, rates(): loss, gained = lax.map(item_rates, jnp.arange(items))  96.7 us
    all_gather x4, blocking collectives, rates(): every_n = lax.all_gather(occ_n, 'kel', axis=0, tiled=True)  75.5 us
    reduce_sum x96, other arithmetic, item_rates(): plain = jnp.sum(table, axis=(0, 2))  72.4 us
    dot_general x48, matrix products, item_rates(): lower = jnp.einsum('bmij,mj->bi', table, chosen, precision=hp)  49.4 us
    dot_general x48, matrix products, item_rates(): upper = jnp.einsum('bmij,mj->bi', table, 1.0 + 2.0 * chosen, precision=hp)  47.8 us
    dot_general x48, matrix products, item_rates(): toward = jnp.einsum('bmij,bi->mj', table, occ_plane, precision=hp)  45.1 us
    dynamic_slice x60, local copies, waits for them, and re-layouts, body(): strength = lax.map(couple, jnp.arange(items))  35.7 us
  transfers between devices with their start and end apart: 5, of which 1 were waited for; matrix products, arithmetic and copies ran while one was open for 42% of the time, Pallas kernels for 0%

commit v1 on v0

v1 whole, which is shorter than its diff:
```python
import functools
import jax
import jax.numpy as jnp
from jax import lax
from jax.experimental import pallas as pl
from jax.experimental.pallas import tpu as pltpu
from jax.sharding import PartitionSpec as P

STEPS = 2
HALF = 0.25
FULL = 0.5
MESH = pl.DeviceIdType.MESH
f32 = jnp.float32
bf16 = jnp.bfloat16


def iota(shape, dim):
    return lax.broadcasted_iota(jnp.int32, shape, dim)


def kernel(
    n, bands, modes, kp, qp, slots, ws,
    elec, phon, ew, pw, coup, ids, counts, speed,
    elec_out, phon_out,
    coup_v, amp, table, feats, init, chosen, msgs, rims,
    rows_s, lanes_s, plain_s, toward_s, nbase, nk1, fbase, fk1, fnow, onehot,
    csem, fsend, frecv, isend, irecv, msend, mrecv, rsend, rrecv,
):
    me = lax.axis_index("kel")
    nbi = bands * kp
    npj = slots * qp
    nmj = modes * qp
    width = init.shape[2]
    bits = n.bit_length() - 1

    def load_coupling(b):
        span = pl.ds(b * modes, modes)
        return pltpu.make_async_copy(coup.at[span], coup_v.at[span], csem.at[b])

    for b in range(bands):
        load_coupling(b).start()

    feats[me] = jnp.concatenate([pw[0], pw[1]], axis=1)
    own = jnp.zeros((8, width), f32)
    rows = iota((8, width), 0)
    lanes = iota((8, width), 1)
    for p in range(slots):
        own = jnp.where((rows == 2) & (lanes == me * 16 + p), (ids[0, p] + 1).astype(f32), own)
    init[me] = own
    for q in range(2):
        for m in range(modes):
            init[me, q : q + 1, m * qp : (m + 1) * qp] = phon[q, m : m + 1, :]
    for b in range(bands):
        init[me, 3:4, b * kp : (b + 1) * kp] = elec[0, b : b + 1, :]

    barrier = pltpu.get_barrier_semaphore()

    def greet(k, _):
        pl.semaphore_signal(
            barrier, inc=1, device_id={"kel": lax.rem(me + k, n)}, device_id_type=MESH
        )
        return 0

    lax.fori_loop(1, n, greet, 0)
    pl.semaphore_wait(barrier, n - 1)

    def partner(bit):
        step = 1 << bit
        return me + step * (1 - 2 * lax.rem(me // step, 2))

    def sends(level):
        bit = bits - 1 - level
        low = 1 << (bit + 1)
        base = lax.rem(me, low)
        return [base + low * t for t in range(1 << level)], partner(bit)

    def ring_copy(ref, ssem, rsem, block, sem, dst):
        return pltpu.make_async_remote_copy(
            src_ref=ref.at[block], dst_ref=ref.at[block],
            send_sem=ssem.at[sem], recv_sem=rsem.at[block],
            device_id={"kel": dst}, device_id_type=MESH)

    def start_level(level):
        blocks, dst = sends(level)
        for t, block in enumerate(blocks):
            sem = (1 << level) - 1 + t
            ring_copy(feats, fsend, frecv, block, sem, dst).start()
            ring_copy(init, isend, irecv, block, sem, dst).start()

    def wait_level(level):
        bit = bits - 1 - level
        low = 1 << (bit + 1)
        dst = partner(bit)
        base = lax.rem(dst, low)
        for t in range(1 << level):
            ring_copy(feats, fsend, frecv, base + low * t, 0, dst).wait_recv()
            ring_copy(init, isend, irecv, base + low * t, 0, dst).wait_recv()

    start_level(0)

    ewt = jnp.transpose(ew[0].astype(f32)).astype(bf16)

    def amps(b, _):
        load_coupling(b).wait()
        for m in range(modes):
            a = jnp.dot(ewt, coup_v[b * modes + m], preferred_element_type=f32)
            amp[m, pl.ds(pl.multiple_of(b * kp, kp), kp), :] = a.astype(bf16)
        return 0

    share = -(-bands // bits)
    done = 0
    for level in range(bits):
        stop = min(bands, done + share)
        lax.fori_loop(done, stop, amps, 0)
        done = stop
        wait_level(level)
        if level + 1 < bits:
            start_level(level + 1)
    for level in range(bits):
        blocks, dst = sends(level)
        for t, block in enumerate(blocks):
            sem = (1 << level) - 1 + t
            ring_copy(feats, fsend, frecv, block, sem, dst).wait_send()
            ring_copy(init, isend, irecv, block, sem, dst).wait_send()

    count = counts[0]
    src = iota((4 * qp, 2 * qp), 0)
    dst_l = iota((4 * qp, 2 * qp), 1)
    for k in range(slots // 2):
        q0, q1 = ids[0, 2 * k], ids[0, 2 * k + 1]
        both = jnp.concatenate([feats[q0 // 2], feats[q1 // 2]], axis=1)
        first = (dst_l < qp) & (src == dst_l + lax.rem(q0, 2) * qp) & (2 * k < count)
        second = (dst_l >= qp) & (src == dst_l + (1 + lax.rem(q1, 2)) * qp) & (2 * k + 1 < count)
        pick = jnp.where(first | second, 1.0, 0.0).astype(bf16)
        chosen[:, k * 2 * qp : (k + 1) * 2 * qp] = jnp.dot(
            both, pick, preferred_element_type=f32).astype(bf16)

    chunk = 128

    def strengths(t, _):
        m = t // (nbi // chunk)
        r = pl.ds(pl.multiple_of(lax.rem(t, nbi // chunk) * chunk, chunk), chunk)
        field = jnp.dot(amp[m, r, :], chosen[...], preferred_element_type=f32)
        table[m, r, :] = (field * field).astype(bf16)
        return 0

    lax.fori_loop(0, modes * nbi // chunk, strengths, 0)

    heads = init[0, 2:3, :]
    for x in range(1, n):
        heads = heads + init[x, 2:3, :]
    wide = n * 16
    heads = heads[:, :wide]
    row = iota((16, wide), 0)
    want = jnp.full((16, wide), -1.0, f32)
    for p in range(slots):
        want = jnp.where(row == p, (ids[0, p] + 1).astype(f32), want)
    for q in range(2):
        want = jnp.where(row == slots + q, (2 * me + q + 1).astype(f32), want)
    onehot[...] = jnp.where(want == heads, 1.0, 0.0).astype(bf16)

    nbase[...] = jnp.zeros_like(nbase)
    for p in range(slots):
        q = ids[0, p]
        two = init[q // 2]
        nbase[p : p + 1, :] = jnp.where(lax.rem(q, 2) == 0, two[0:1, :nmj], two[1:2, :nmj])
    for q in range(2):
        nbase[slots + q : slots + q + 1, :] = init[me, q : q + 1, :nmj]
    rows_s[...] = nbase[...]
    nk1[...] = jnp.zeros_like(nk1)
    fbase[...] = init[me, 3:4, :nbi]
    fnow[...] = init[me, 3:4, :nbi]
    fk1[...] = jnp.zeros_like(fk1)
    before = lax.rem(me + n - 1, n)
    after = lax.rem(me + 1, n)
    rims[0] = jnp.broadcast_to(init[before, 3:4, :nbi], (8, nbi))

    lane = iota((1, nbi), 1)
    drift = jnp.zeros((1, nbi), f32)
    for b in range(bands):
        drift = jnp.where(lane // kp == b, speed[b], drift)
    half_lane = iota((1, 2 * qp), 1) < qp

    def send_msg(e, k):
        dst = lax.rem(me + k, n)
        return pltpu.make_async_remote_copy(
            src_ref=msgs.at[e, me], dst_ref=msgs.at[e, me],
            send_sem=msend.at[e, k], recv_sem=mrecv.at[e, me],
            device_id={"kel": dst}, device_id_type=MESH)

    def take_msg(e, k):
        src_d = lax.rem(me + n - k, n)
        return pltpu.make_async_remote_copy(
            src_ref=msgs.at[e, src_d], dst_ref=msgs.at[e, src_d],
            send_sem=msend.at[e, k], recv_sem=mrecv.at[e, src_d],
            device_id={"kel": src_d}, device_id_type=MESH)

    def rim_copy(e):
        return pltpu.make_async_remote_copy(
            src_ref=rims.at[2 * STEPS + 1 + e], dst_ref=rims.at[e + 1],
            send_sem=rsend.at[e], recv_sem=rrecv.at[e],
            device_id={"kel": after}, device_id_type=MESH)

    def split(x):
        hi = x.astype(bf16).astype(f32)
        return hi, x - hi

    def triple(hi, lo, shape):
        r = iota(shape, 0)
        return jnp.where(r == 0, hi, jnp.where(r == 1, lo, jnp.where(r == 2, 1.0, 0.0))).astype(bf16)

    def evaluate(e, _):
        even = lax.rem(e, 2) == 0
        for mm in range(modes // 2):
            here = rows_s[:, 2 * mm * qp : 2 * (mm + 1) * qp]
            turn = pltpu.roll(here, qp, 1)
            for k in range(slots // 2):
                cols = slice(2 * k * qp, 2 * (k + 1) * qp)
                lanes_s[2 * mm : 2 * mm + 1, cols] = jnp.where(
                    half_lane, here[2 * k : 2 * k + 1], turn[2 * k + 1 : 2 * k + 2])
                lanes_s[2 * mm + 1 : 2 * mm + 2, cols] = jnp.where(
                    half_lane, turn[2 * k : 2 * k + 1], here[2 * k + 1 : 2 * k + 2])
        occ = fnow[...]
        fhi, flo = split(occ)
        fmat = triple(fhi, flo, (8, nbi))
        low = jnp.zeros((8, nbi), f32)
        for m in range(modes):
            tab = table[m]
            tow = jnp.dot(fmat, tab, preferred_element_type=f32)
            toward_s[m : m + 1, :] = tow[0:1] + tow[1:2]
            plain_s[m : m + 1, :] = tow[2:3]
            nhi, nlo = split(lanes_s[m : m + 1, :])
            low = low + lax.dot_general(
                triple(nhi, nlo, (8, npj)), tab, (((1,), (1,)), ((), ())),
                preferred_element_type=f32)
        nl = lanes_s[0:modes, :]
        gained = (1.0 + 2.0 * nl) * toward_s[0:modes, :] - nl * plain_s[0:modes, :]
        for k in range(slots // 2):
            here = gained[:, 2 * k * qp : 2 * (k + 1) * qp]
            turn = pltpu.roll(here, qp, 1)
            for mm in range(modes // 2):
                cols = slice(2 * mm * qp, 2 * (mm + 1) * qp)
                rows_s[2 * k : 2 * k + 1, cols] = jnp.where(
                    half_lane, here[2 * mm : 2 * mm + 1], turn[2 * mm + 1 : 2 * mm + 2])
                rows_s[2 * k + 1 : 2 * k + 2, cols] = jnp.where(
                    half_lane, turn[2 * mm : 2 * mm + 1], here[2 * mm + 1 : 2 * mm + 2])
        live = iota((16, nmj), 0) < slots
        msgs[e, me] = jnp.where(live, rows_s[...], 0.0).astype(bf16)

        def go(k, _):
            send_msg(e, k).start()
            return 0

        lax.fori_loop(1, n, go, 0)

        lower = low[0:1] + low[1:2]
        loss = occ * (low[2:3] + 2.0 * lower) - lower
        ke = -loss / (slots * modes * qp) - drift * (occ - rims[e, 0:1, :])
        nextf = fbase[...] + HALF * (jnp.where(even, ke, fk1[...]) + ke)
        fk1[...] = ke
        fbase[...] = jnp.where(even, fbase[...], nextf)
        fnow[...] = nextf
        rims[2 * STEPS + 1 + e] = jnp.broadcast_to(nextf, (8, nbi))
        rim_copy(e).start()

        def come(k, _):
            take_msg(e, k).wait_recv()
            return 0

        lax.fori_loop(1, n, come, 0)
        every = msgs[e].reshape(n * 16, nmj)
        kn = jnp.dot(onehot[...], every, preferred_element_type=f32) / (slots * bands * kp)
        nextn = nbase[...] + HALF * (jnp.where(even, kn, nk1[...]) + kn)
        nk1[...] = kn
        nbase[...] = jnp.where(even, nbase[...], nextn)
        rows_s[...] = nextn
        rim_copy(e).wait_recv()
        return 0

    lax.fori_loop(0, 2 * STEPS, evaluate, 0)

    for b in range(bands):
        elec_out[0, b : b + 1, :] = fnow[:, b * kp : (b + 1) * kp]
    for q in range(2):
        for m in range(modes):
            phon_out[q, m : m + 1, :] = rows_s[slots + q : slots + q + 1, m * qp : (m + 1) * qp]

    def settle(e, _):
        def gone(k, _):
            send_msg(e, k).wait_send()
            return 0

        lax.fori_loop(1, n, gone, 0)
        rim_copy(e).wait_send()
        return 0

    lax.fori_loop(0, 2 * STEPS, settle, 0)


def body(n, electrons, phonons, elec_wannier, phon_wannier, coupling, pair_blocks, pair_counts, drift_speed):
    _, bands, kp = electrons.shape
    _, modes, qp = phonons.shape
    slots = pair_blocks.shape[1]
    ws = elec_wannier.shape[1]
    nbi, npj, nmj = bands * kp, slots * qp, modes * qp
    width = max(nbi, n * 16, nmj)
    evals = 2 * STEPS
    vmem = pl.BlockSpec(memory_space=pltpu.VMEM)
    smem = pl.BlockSpec(memory_space=pltpu.SMEM)
    dma = pltpu.SemaphoreType.DMA
    return pl.pallas_call(
        functools.partial(kernel, n, bands, modes, kp, qp, slots, ws),
        out_shape=(
            jax.ShapeDtypeStruct(electrons.shape, f32),
            jax.ShapeDtypeStruct(phonons.shape, f32),
        ),
        in_specs=[vmem, vmem, vmem, vmem, pl.BlockSpec(memory_space=pl.ANY), smem, smem, smem],
        out_specs=(vmem, vmem),
        scratch_shapes=[
            pltpu.VMEM(coupling.shape, bf16),
            pltpu.VMEM((modes, nbi, ws), bf16),
            pltpu.VMEM((modes, nbi, npj), bf16),
            pltpu.VMEM((n, ws, 2 * qp), bf16),
            pltpu.VMEM((n, 8, width), f32),
            pltpu.VMEM((ws, npj), bf16),
            pltpu.VMEM((evals, n, 16, nmj), bf16),
            pltpu.VMEM((2 * evals + 1, 8, nbi), f32),
            pltpu.VMEM((16, nmj), f32),
            pltpu.VMEM((8, npj), f32),
            pltpu.VMEM((8, npj), f32),
            pltpu.VMEM((8, npj), f32),
            pltpu.VMEM((16, nmj), f32),
            pltpu.VMEM((16, nmj), f32),
            pltpu.VMEM((1, nbi), f32),
            pltpu.VMEM((1, nbi), f32),
            pltpu.VMEM((1, nbi), f32),
            pltpu.VMEM((16, n * 16), bf16),
            dma((bands,)),
            dma((n,)), dma((n,)), dma((n,)), dma((n,)),
            dma((evals, n)), dma((evals, n)),
            dma((evals,)), dma((evals,)),
        ],
        compiler_params=pltpu.CompilerParams(
            collective_id=0, has_side_effects=True, vmem_limit_bytes=40 * 2**20),
    )(electrons, phonons, elec_wannier, phon_wannier, coupling, pair_blocks, pair_counts, drift_speed)


def solution(mesh):
    rows3 = P(("groups", "kel"), None, None)
    placed = (rows3, rows3, rows3, rows3, P(), P(("groups", "kel"), None), P(("groups", "kel")), P("groups"))
    return jax.shard_map(
        functools.partial(body, mesh.shape["kel"]),
        mesh=mesh, in_specs=placed, out_specs=(rows3, rows3), check_vma=False)
```

time: 828 us -> 80.3 us (0.10)
  blocking collectives: 323 us -> 0 us
  matrix products: 175 us -> 0 us
  loops' own time: 119 us -> 0 us
  other arithmetic: 105 us -> 0 us
  Pallas kernels: 0 us -> 70.1 us
  local copies, waits for them, and re-layouts: 69.5 us -> 8.49 us
  between operations: 15.5 us -> 1.31 us
  waiting for transfers between devices: 11.5 us -> 0 us
    unnamed x4 -> x0, blocking collectives: 248 us -> none
    dot_general x161 -> x0, matrix products: 175 us -> none  [the longest x48 49.4 us: item_rates(): lower = jnp.einsum('bmij,mj->bi', table, chosen, precision=hp)]
    another operation x5 -> x0, loops' own time: 119 us -> none  [the longest x4 96.7 us: rates(): loss, gained = lax.map(item_rates, jnp.arange(items))]
    all_gather x4 -> x0, blocking collectives: 75.5 us -> none  [rates(): every_n = lax.all_gather(occ_n, 'kel', axis=0, tiled=True)]
    reduce_sum x100 -> x0, other arithmetic: 72.4 us -> none  [the longest x96 72.4 us: item_rates(): plain = jnp.sum(table, axis=(0, 2))]
    pallas_call x0 -> x1, Pallas kernels: none -> 70.1 us  [body(): pl.pallas_call(functools.partial(kernel, n, bands, modes, kp, qp, slots,...]
    dynamic_slice x72 -> x0, local copies, waits for them, and re-layouts: 43.4 us -> none  [the longest x60 35.7 us: body(): strength = lax.map(couple, jnp.arange(items))]
    dynamic_update_slice x48 -> x0, other arithmetic: 26.1 us -> none  [rates(): loss, gained = lax.map(item_rates, jnp.arange(items))]
  transfers between devices with their start and end apart: 5 -> 0, of which waited for: 1 -> 0; matrix products, arithmetic and copies ran while one was open for 42% -> 0% of each run, Pallas kernels for 0% -> 0%
where the time goes in v1:
time: 80.3 us; the launch traced here: 79.9 us
  Pallas kernels  70.1 us (87%)
  local copies, waits for them, and re-layouts  8.49 us (11%)
  between operations  1.31 us (2%)
    pallas_call x1, Pallas kernels, body(): pl.pallas_call(functools.partial(kernel, n, bands, modes, kp, qp, slots,...  70.1 us
    unnamed x12, local copies, waits for them, and re-layouts  7.9 us

profile of v1, /device:TPU:0, one launch (start us, length us, event | category | flops | bytes accessed | tf_op | source)
XLA Modules:
  0.0 79.9 jit_solution(12329111067543069662)
XLA Ops:
  1.3 0.7 copy.10.phon
  2.0 0.9 %copy.11.ew = bf16[1,256,64]{2,1,0:T(8,128)(2,1)S(1)} copy(bf16[1,256,64]{1,2,0:T(8,128)(2,1)} %param.10) | data formatting | bytes 65536 | tf_op args[2]
  2.8 1.0 %copy.12.pw = bf16[2,256,64]{2,1,0:T(8,128)(2,1)S(1)} copy(bf16[2,256,64]{1,2,0:T(8,128)(2,1)} %param.11) | data formatting | bytes 131072 | tf_op args[3]
  3.8 0.0 copy-start
  3.8 2.8 %copy-done = bf16[48,256,256]{2,1,0:T(8,128)(2,1)S(1)} copy-done((bf16[48,256,256]{2,1,0:T(8,128)(2,1)S(1)}, bf16[48,256,256]{2,1,0:T(8,128)(2,1)}, u32[]{:S(2)}) %copy-start) | copy-done | bytes 6291480
  6.6 0.0 copy-start.1
  6.6 0.7 copy-done.1
  7.3 0.0 copy-start.2
  7.3 0.7 copy-done.2
  7.9 0.0 copy-start.3
  7.9 0.7 copy-done.3
  8.6 70.1 %shard_map.95 = (f32[1,8,64]{2,1,0:T(8,128)S(1)}, f32[2,6,64]{2,1,0:T(8,128)S(1)}) custom-call(f32[1,8,64]{2,1,0:T(8,128)S(1)} %copy-done.1, f32[2,6,64]{2,1,0:T(8,128)S(1)} %copy.10.phon, bf16[1,256,64]{2,1,0:T(8,128)(2,1)S(1)} %copy.11.ew, bf16[2,256,64]{2,1,0:T(8,128)(2,1)S(1)} %copy.12.pw, bf16[48,256,256]{2,1,0:T(8,128)(2,1)S(1)} %copy-done, ...), custom_call_target="tpu_custom_call" | custom-call | tf_op jit(solution)/shard_map/pallas_call | solution.py:311
  78.7 0.6 copy.13
  79.3 0.6 copy.16
Async XLA Ops:
  3.8 2.8 %copy-start = (bf16[48,256,256]{2,1,0:T(8,128)(2,1)S(1)}, bf16[48,256,256]{2,1,0:T(8,128)(2,1)}, u32[]{:S(2)}) copy-start(bf16[48,256,256]{2,1,0:T(8,128)(2,1)} %coup.1) | copy-start | bytes 18874372
  6.6 0.7 copy-start.1
  7.3 0.7 copy-start.2
  7.9 0.7 copy-start.3

commit v2 on v1

v2 whole, which is shorter than its diff:
```python
import functools
import jax
import jax.numpy as jnp
from jax import lax
from jax.experimental import pallas as pl
from jax.experimental.pallas import tpu as pltpu
from jax.sharding import PartitionSpec as P

STEPS = 2
HALF = 0.25
FULL = 0.5
MESH = pl.DeviceIdType.MESH
f32 = jnp.float32
bf16 = jnp.bfloat16


def iota(shape, dim):
    return lax.broadcasted_iota(jnp.int32, shape, dim)


def kernel(
    n, bands, modes, kp, qp, slots, ws,
    elec, phon, ew, pw, coup, ids_h, counts_h, speed_h,
    elec_out, phon_out,
    coup_v, amp, table, feats, init, chosen, msgs, rims,
    rows_s, trow, prow, lanes_s, plain_s, toward_s, nbase, nk1, fbase, fk1, fnow, onehot,
    ewt, elec_v, phon_v, ids, counts, speed,
    csem, asem, fsend, frecv, isend, irecv, msend, mrecv, rsend, rrecv,
):
    me = lax.axis_index("kel")
    nbi = bands * kp
    npj = slots * qp
    nmj = modes * qp
    width = init.shape[2]
    bits = n.bit_length() - 1
    chips = n // 2
    mate = me + 1 - 2 * lax.rem(me, 2)

    small = [
        pltpu.make_async_copy(x, y, asem.at[i])
        for i, (x, y) in enumerate((
            (ids_h, ids), (phon, phon_v), (elec, elec_v), (pw, feats.at[pl.ds(2 * me, 2)]),
            (ew, ewt), (counts_h, counts), (speed_h, speed)))
    ]
    for copy in small:
        copy.start()

    def load_coupling(b):
        span = pl.ds(b * modes, modes)
        return pltpu.make_async_copy(coup.at[span], coup_v.at[span], csem.at[b])

    for b in range(bands):
        load_coupling(b).start()

    barrier = pltpu.get_barrier_semaphore()

    def partner(bit):
        step = 1 << bit
        return me + step * (1 - 2 * lax.rem(me // step, 2))

    for bit in range(bits):
        pl.semaphore_signal(
            barrier, inc=1, device_id={"kel": partner(bit)}, device_id_type=MESH)

    for copy in small:
        copy.wait()
    own = jnp.zeros((4, width), f32)
    rows = iota((4, width), 0)
    lanes = iota((4, width), 1)
    for p in range(slots):
        own = jnp.where((rows == 2) & (lanes == me * 16 + p), (ids[0, p] + 1).astype(f32), own)
    init[me] = own
    for q in range(2):
        for m in range(modes):
            init[me, q : q + 1, m * qp : (m + 1) * qp] = phon_v[m, q : q + 1, :]
    for b in range(bands):
        init[me, 3:4, b * kp : (b + 1) * kp] = elec_v[0, b : b + 1, :]
    pl.semaphore_wait(barrier, bits)

    def tree_copies(flips, bit):
        block = me
        for other in flips:
            block = block + partner(other) - me
        return [
            pltpu.make_async_remote_copy(
                src_ref=ref.at[where], dst_ref=ref.at[where],
                send_sem=ssem.at[sum(1 << x for x in flips) + (1 << bit)], recv_sem=rsem.at[block],
                device_id={"kel": partner(bit)}, device_id_type=MESH)
            for ref, where, ssem, rsem in (
                (feats, pl.ds(2 * block, 2), fsend, frecv), (init, block, isend, irecv))
        ]

    subsets = [[bit for bit in range(bits) if v >> bit & 1] for v in range(n)]
    subsets.sort(key=lambda flips: (len(flips), min(flips + [bits]) == 0, -sum(1 << x for x in flips)))

    def pass_on(flips):
        for bit in range(min(flips + [bits]) - 1, -1, -1):
            for copy in tree_copies(flips, bit):
                copy.start()

    pass_on([])

    def amps(b, _):
        load_coupling(b).wait()
        for m in range(modes):
            a = jnp.dot(ewt[0], coup_v[b * modes + m], preferred_element_type=f32)
            amp[m, pl.ds(pl.multiple_of(b * kp, kp), kp), :] = a.astype(bf16)
        return 0

    done = 0
    for flips in subsets[1:]:
        if done < bands:
            lax.fori_loop(done, min(bands, done + 2), amps, 0)
            done += 2
        for copy in tree_copies(flips, min(flips)):
            copy.wait_recv()
        pass_on(flips)
    if done < bands:
        lax.fori_loop(done, bands, amps, 0)

    count = counts[0]
    for k in range(slots // 2):
        pair = [
            jnp.where(2 * k + i < count, feats[ids[0, 2 * k + i]].astype(f32), 0.0) for i in range(2)
        ]
        chosen[:, k * 2 * qp : (k + 1) * 2 * qp] = jnp.transpose(
            jnp.concatenate(pair, axis=0)).astype(bf16)

    chunk = nbi

    def strengths(t, _):
        m = t // (nbi // chunk)
        r = pl.ds(pl.multiple_of(lax.rem(t, nbi // chunk) * chunk, chunk), chunk)
        field = jnp.dot(amp[m, r, :], chosen[...], preferred_element_type=f32)
        table[m, r, :] = (field * field).astype(bf16)
        return 0

    lax.fori_loop(0, modes * nbi // chunk, strengths, 0)

    heads = init[0, 2:3, :]
    for x in range(1, n):
        heads = heads + init[x, 2:3, :]
    wide = n * 16
    heads = heads[:, :wide]
    row = iota((16, wide), 0)
    want = jnp.full((16, wide), -1.0, f32)
    for p in range(slots):
        want = jnp.where(row == p, (ids[0, p] + 1).astype(f32), want)
    for q in range(2):
        want = jnp.where(row == slots + q, (2 * me + q + 1).astype(f32), want)
    onehot[...] = jnp.where(want == heads, 1.0, 0.0).astype(bf16)

    nbase[...] = jnp.zeros_like(nbase)
    for p in range(slots):
        q = ids[0, p]
        two = init[q // 2]
        nbase[p : p + 1, :] = jnp.where(lax.rem(q, 2) == 0, two[0:1, :nmj], two[1:2, :nmj])
    for q in range(2):
        nbase[slots + q : slots + q + 1, :] = init[me, q : q + 1, :nmj]
    rows_s[...] = nbase[...]
    nk1[...] = jnp.zeros_like(nk1)
    fbase[...] = init[me, 3:4, :nbi]
    fnow[...] = init[me, 3:4, :nbi]
    fk1[...] = jnp.zeros_like(fk1)
    before = lax.rem(me + n - 1, n)
    after = lax.rem(me + 1, n)
    rims[0] = init[before, 3:4, :nbi]

    lane = iota((1, nbi), 1)
    drift = jnp.zeros((1, nbi), f32)
    for b in range(bands):
        drift = jnp.where(lane // kp == b, speed[b], drift)
    half_lane = iota((1, 2 * qp), 1) < qp

    def msg_copy(e, block, sem, dst):
        return pltpu.make_async_remote_copy(
            src_ref=msgs.at[e, block], dst_ref=msgs.at[e, block],
            send_sem=msend.at[e, sem], recv_sem=mrecv.at[e, block],
            device_id={"kel": dst}, device_id_type=MESH)

    def spread(e, k):
        return msg_copy(e, me, k, lax.rem(me + 2 * k, n))

    def arrive(e, k):
        return msg_copy(e, lax.rem(me + n - 2 * k, n), k, mate)

    def forward(e, k):
        return msg_copy(e, lax.rem(me + n - 2 * k, n), chips + k, mate)

    def relayed(e, k):
        return msg_copy(e, lax.rem(mate + n - 2 * k, n), k, mate)

    def rim_copy(e):
        return pltpu.make_async_remote_copy(
            src_ref=rims.at[2 * STEPS + e], dst_ref=rims.at[e + 1],
            send_sem=rsend.at[e], recv_sem=rrecv.at[e],
            device_id={"kel": after}, device_id_type=MESH)

    def split(x):
        hi = x.astype(bf16).astype(f32)
        return hi, x - hi

    def triple(hi, lo, shape):
        r = iota(shape, 0)
        return jnp.where(r == 0, hi, jnp.where(r == 1, lo, jnp.where(r == 2, 1.0, 0.0))).astype(bf16)

    def to_rows(src_ref, dst_ref):
        for k in range(slots // 2):
            here = src_ref[:, 2 * k * qp : 2 * (k + 1) * qp]
            turn = pltpu.roll(here, qp, 1)
            for mm in range(modes // 2):
                cols = slice(2 * mm * qp, 2 * (mm + 1) * qp)
                dst_ref[2 * k : 2 * k + 1, cols] = jnp.where(
                    half_lane, here[2 * mm : 2 * mm + 1], turn[2 * mm + 1 : 2 * mm + 2])
                dst_ref[2 * k + 1 : 2 * k + 2, cols] = jnp.where(
                    half_lane, turn[2 * mm : 2 * mm + 1], here[2 * mm + 1 : 2 * mm + 2])

    def to_lanes(src_ref, dst_ref):
        for mm in range(modes // 2):
            here = src_ref[:, 2 * mm * qp : 2 * (mm + 1) * qp]
            turn = pltpu.roll(here, qp, 1)
            for k in range(slots // 2):
                cols = slice(2 * k * qp, 2 * (k + 1) * qp)
                dst_ref[2 * mm : 2 * mm + 1, cols] = jnp.where(
                    half_lane, here[2 * k : 2 * k + 1], turn[2 * k + 1 : 2 * k + 2])
                dst_ref[2 * mm + 1 : 2 * mm + 2, cols] = jnp.where(
                    half_lane, turn[2 * k : 2 * k + 1], here[2 * k + 1 : 2 * k + 2])

    def toward_of(occ):
        fhi, flo = split(occ)
        fmat = triple(fhi, flo, (8, nbi))
        for m in range(modes):
            tow = jnp.dot(fmat, table[m], preferred_element_type=f32)
            toward_s[m : m + 1, :] = tow[0:1] + tow[1:2]
            plain_s[m : m + 1, :] = tow[2:3]
        to_rows(toward_s, trow)

    trow[...] = jnp.zeros_like(trow)
    prow[...] = jnp.zeros_like(prow)
    toward_of(fnow[...])
    to_rows(plain_s, prow)
    evals = 2 * STEPS

    def evaluate(e, _):
        even = lax.rem(e, 2) == 0
        occ_n = rows_s[...]
        gained = (1.0 + 2.0 * occ_n) * trow[...] - occ_n * prow[...]
        msgs[e, me] = gained.astype(bf16)
        for k in range(1, chips):
            spread(e, k).start()
        msg_copy(e, me, 0, mate).start()

        to_lanes(rows_s, lanes_s)
        low = jnp.zeros((8, nbi), f32)
        for m in range(modes):
            nhi, nlo = split(lanes_s[m : m + 1, :])
            low = low + lax.dot_general(
                triple(nhi, nlo, (8, npj)), table[m], (((1,), (1,)), ((), ())),
                preferred_element_type=f32)
        lower = low[0:1] + low[1:2]
        occ = fnow[...]
        loss = occ * (low[2:3] + 2.0 * lower) - lower

        @pl.when(e > 0)
        def _():
            rim_copy(e - 1).wait_recv()

        ke = -loss / (slots * modes * qp) - drift * (occ - rims[e])
        nextf = fbase[...] + HALF * (jnp.where(even, ke, fk1[...]) + ke)
        fk1[...] = ke
        fbase[...] = jnp.where(even, fbase[...], nextf)
        fnow[...] = nextf

        @pl.when(e < evals - 1)
        def _():
            rims[evals + e] = nextf
            rim_copy(e).start()
            toward_of(nextf)

        for k in range(1, chips):
            arrive(e, k).wait_recv()
            forward(e, k).start()
        for k in range(chips):
            relayed(e, k).wait_recv()
        every = msgs[e].reshape(n * 16, nmj)
        kn = jnp.dot(onehot[...], every, preferred_element_type=f32) / (slots * bands * kp)
        nextn = nbase[...] + HALF * (jnp.where(even, kn, nk1[...]) + kn)
        nk1[...] = kn
        nbase[...] = jnp.where(even, nbase[...], nextn)
        rows_s[...] = nextn
        return 0

    lax.fori_loop(0, evals, evaluate, 0)

    for b in range(bands):
        elec_out[0, b : b + 1, :] = fnow[:, b * kp : (b + 1) * kp]
    for q in range(2):
        for m in range(modes):
            phon_out[m, q : q + 1, :] = rows_s[slots + q : slots + q + 1, m * qp : (m + 1) * qp]

    def settle(e, _):
        msg_copy(e, me, 0, mate).wait_send()
        for k in range(1, chips):
            spread(e, k).wait_send()
            forward(e, k).wait_send()
        return 0

    lax.fori_loop(0, evals, settle, 0)
    for e in range(evals - 1):
        rim_copy(e).wait_send()
    for flips in subsets:
        for bit in range(min(flips + [bits])):
            for copy in tree_copies(flips, bit):
                copy.wait_send()


def body(n, electrons, phonons, elec_wannier, phon_wannier, coupling, pair_blocks, pair_counts, drift_speed):
    _, bands, kp = electrons.shape
    _, modes, qp = phonons.shape
    slots = pair_blocks.shape[1]
    ws = elec_wannier.shape[1]
    nbi, npj, nmj = bands * kp, slots * qp, modes * qp
    width = max(nbi, n * 16, nmj)
    evals = 2 * STEPS
    vmem = pl.BlockSpec(memory_space=pltpu.VMEM)
    dma = pltpu.SemaphoreType.DMA
    elec_o, phon_o = pl.pallas_call(
        functools.partial(kernel, n, bands, modes, kp, qp, slots, ws),
        out_shape=(
            jax.ShapeDtypeStruct(electrons.shape, f32),
            jax.ShapeDtypeStruct((modes, 2, qp), f32),
        ),
        in_specs=[pl.BlockSpec(memory_space=pltpu.HBM)] * 8,
        out_specs=(vmem, vmem),
        scratch_shapes=[
            pltpu.VMEM(coupling.shape, bf16),
            pltpu.VMEM((modes, nbi, ws), bf16),
            pltpu.VMEM((modes, nbi, npj), bf16),
            pltpu.VMEM((2 * n, qp, ws), bf16),
            pltpu.VMEM((n, 4, width), f32),
            pltpu.VMEM((ws, npj), bf16),
            pltpu.VMEM((evals, n, 16, nmj), bf16),
            pltpu.VMEM((2 * evals - 1, 1, nbi), f32),
            pltpu.VMEM((16, nmj), f32),
            pltpu.VMEM((16, nmj), f32),
            pltpu.VMEM((16, nmj), f32),
            pltpu.VMEM((8, npj), f32),
            pltpu.VMEM((8, npj), f32),
            pltpu.VMEM((8, npj), f32),
            pltpu.VMEM((16, nmj), f32),
            pltpu.VMEM((16, nmj), f32),
            pltpu.VMEM((1, nbi), f32),
            pltpu.VMEM((1, nbi), f32),
            pltpu.VMEM((1, nbi), f32),
            pltpu.VMEM((16, n * 16), bf16),
            pltpu.VMEM((1, kp, ws), bf16),
            pltpu.VMEM(electrons.shape, f32),
            pltpu.VMEM((modes, 2, qp), f32),
            pltpu.SMEM(pair_blocks.shape, jnp.int32),
            pltpu.SMEM(pair_counts.shape, jnp.int32),
            pltpu.SMEM(drift_speed.shape, f32),
            dma((bands,)), dma((7,)),
            dma((n,)), dma((n,)), dma((n,)), dma((n,)),
            dma((evals, n)), dma((evals, n)),
            dma((evals,)), dma((evals,)),
        ],
        compiler_params=pltpu.CompilerParams(
            collective_id=0, has_side_effects=True, vmem_limit_bytes=60 * 2**20),
    )(
        electrons, jnp.transpose(phonons, (1, 0, 2)), jnp.swapaxes(elec_wannier, 1, 2),
        jnp.swapaxes(phon_wannier, 1, 2), coupling, pair_blocks, pair_counts, drift_speed)
    return elec_o, jnp.transpose(phon_o, (1, 0, 2))


def solution(mesh):
    rows3 = P(("groups", "kel"), None, None)
    placed = (rows3, rows3, rows3, rows3, P(), P(("groups", "kel"), None), P(("groups", "kel")), P("groups"))
    return jax.shard_map(
        functools.partial(body, mesh.shape["kel"]),
        mesh=mesh, in_specs=placed, out_specs=(rows3, rows3), check_vma=False)
```

time: 80.3 us -> 49.1 us (0.61)
  Pallas kernels: 70.1 us -> 44.8 us
  local copies, waits for them, and re-layouts: 8.49 us -> 2.55 us
    pallas_call x1, Pallas kernels: 70.1 us -> 44.8 us  [body(): pl.pallas_call(functools.partial(kernel, n, bands, modes, kp, qp, slots,...]
    unnamed x12 -> x2, local copies, waits for them, and re-layouts: 7.9 us -> 2.55 us
where the time goes in v2:
time: 49.1 us; the launch traced here: 48.6 us
  Pallas kernels  44.8 us (91%)
  local copies, waits for them, and re-layouts  2.55 us (5%)
  between operations  1.29 us (3%)
    pallas_call x1, Pallas kernels, body(): pl.pallas_call(functools.partial(kernel, n, bands, modes, kp, qp, slots,...  44.8 us
    unnamed x2, local copies, waits for them, and re-layouts  2.55 us

profile of v2, /device:TPU:0, one launch (start us, length us, event | category | flops | bytes accessed | tf_op | source)
XLA Modules:
  0.0 48.6 jit_solution(7075295866128903671)
XLA Ops:
  1.3 44.8 %shard_map.95 = (f32[1,8,64]{2,1,0:T(8,128)}, f32[6,2,64]{2,1,0:T(2,128)}) custom-call(f32[1,8,64]{2,1,0:T(8,128)} %elec.1, f32[6,2,64]{2,1,0:T(2,128)} %bitcast.7, bf16[1,64,256]{2,1,0:T(8,128)(2,1)} %bitcast.5, bf16[2,64,256]{2,1,0:T(8,128)(2,1)} %bitcast.4, bf16[48,256,256]{2,1,0:T(8,128)(2,1)} %coup.1, s32[1,12]{1,0:T(1,128)} %ids_h.1, ...), custom_call_target="tpu_custom_call" | custom-call | tf_op jit(solution)/shard_map/pallas_call | solution.py:327
  46.1 1.3 %copy.13 = f32[1,8,64]{2,1,0:T(8,128)} copy(f32[1,8,64]{2,1,0:T(8,128)} %get-tuple-element.8) | data formatting | bytes 4096
  47.3 1.3 %copy.14 = f32[2,6,64]{2,0,1:T(2,128)} copy(f32[2,6,64]{2,0,1:T(2,128)} %bitcast.6) | data formatting | bytes 6144
